TPU v7x, 32 devices: a whole 2x2x4 slice. The times are simulated.
32 devices in a mesh: job: 2 (over x), fsdp: 16 (over z, y, core).
Axes of the slice: x: 2, y: 2, z: 4, core: 2. Of those that a mesh axis runs over, the one named last changes fastest.
Arguments:
- decode_input_rows: bfloat16 [32, 2, 5120], P(('job', 'fsdp')), parts along dimension 0, may hold values from -150 to 150
- cached_rotated_keys: bfloat16 [32, 2048, 1024], P(('job', 'fsdp')), parts along dimension 0, may hold values from -4 to 4
- cached_value_rows: bfloat16 [32, 2048, 1024], P(('job', 'fsdp')), parts along dimension 0, may hold values from -5 to 5
- lengths: int32 [32], P(('job', 'fsdp')), parts along dimension 0, may hold values from 1 to 2048, as said below
- base_query_weight: bfloat16 [5120, 8192], P(None, 'fsdp'), may hold values from -0.078125 to 0.078125
- base_key_weight: bfloat16 [5120, 1024], P(None, 'fsdp'), may hold values from -0.078125 to 0.078125
- base_value_weight: bfloat16 [5120, 1024], P(None, 'fsdp'), may hold values from -0.078125 to 0.078125
- base_output_weight: bfloat16 [8192, 5120], P('fsdp'), may hold values from -1.5 to 1.5
- query_adapter_down: bfloat16 [10240, 64], P(('job', 'fsdp')), parts along dimension 0, may hold values from -0.75 to 0.75
- query_adapter_up: bfloat16 [16384, 64], P(('job', 'fsdp')), parts along dimension 0, may hold values from -0.0390625 to 0.0390625
- key_adapter_down: bfloat16 [10240, 64], P(('job', 'fsdp')), parts along dimension 0, may hold values from -0.75 to 0.75
- key_adapter_up: bfloat16 [2048, 64], P(('job', 'fsdp')), parts along dimension 0, may hold values from -0.0390625 to 0.0390625
- value_adapter_down: bfloat16 [10240, 64], P(('job', 'fsdp')), parts along dimension 0, may hold values from -0.75 to 0.75
- value_adapter_up: bfloat16 [2048, 64], P(('job', 'fsdp')), parts along dimension 0, may hold values from -0.0390625 to 0.0390625
- output_adapter_down: bfloat16 [16384, 64], P(('job', 'fsdp')), parts along dimension 0, may hold values from -0.75 to 0.75
- output_adapter_up: bfloat16 [10240, 64], P(('job', 'fsdp')), parts along dimension 0, may hold values from -0.375 to 0.375
Outputs:
- block_out: bfloat16 [32, 2, 5120], P(('job', 'fsdp')), parts along dimension 0
- new_keys: bfloat16 [32, 2, 1024], P(('job', 'fsdp')), parts along dimension 0
- new_values: bfloat16 [32, 2, 1024], P(('job', 'fsdp')), parts along dimension 0
There are 2 independent parts, one for each index of `job`. A program takes and returns all parts, laid end to end along the dimension named above; an argument that names none is the same for every part. Nothing has to cross between parts.
Inputs may be any that keep to these rules, and one draw needn't show every extreme that they name: Row r's cache holds keys and values at positions 0 to lengths[r] - 1, other positions hold unrelated numbers; some row has exactly 2048 and some row exactly 1.
All inputs are finite; a program needn't handle non-finite values.
Results may differ from a plain program's by a relative error of at most 0.014.
Values may be sent and summed in bfloat16 or wider, within the bound.
A program may use at most 128 MiB of HBM per device.

v0:
```python
import math

import jax
import jax.numpy as jnp
from jax import lax
from jax.sharding import PartitionSpec as P

QHEADS = 64
KVHEADS = 8
HEAD = 128
STEPS = 2


SCALE = 2.0
THETA = 1000000.0
EPSILON = 1e-06


def combined_weight_matrix(base, left, right):
    delta = jnp.dot(left, right.T, preferred_element_type=jnp.float32)
    return (base.astype(jnp.float32) + SCALE * delta).astype(jnp.bfloat16)


def rms_rows(values):
    wide = values.astype(jnp.float32)
    return wide * lax.rsqrt(jnp.mean(wide * wide, axis=-1, keepdims=True) + EPSILON)


def rotary(heads, positions):
    half_size = heads.shape[-1] // 2
    frequency = THETA ** (-2.0 * jnp.arange(half_size, dtype=jnp.float32) / heads.shape[-1])
    angles = positions.astype(jnp.float32)[:, None] * frequency[None, :]
    cosine = jnp.cos(angles)[:, None, :]
    sine_part = jnp.sin(angles)[:, None, :]
    first = heads[..., :half_size]
    second = heads[..., half_size:]
    return jnp.concatenate(
        [first * cosine - second * sine_part, second * cosine + first * sine_part], axis=-1
    )


def attend(query_rot, cached_rotated_keys, cached_value_rows, valid, fresh_keys, fresh_values):
    rows_here, length, width = cached_rotated_keys.shape
    groups = width // HEAD
    query = query_rot.reshape(rows_here, groups, -1, HEAD)
    cached_k = cached_rotated_keys.reshape(rows_here, length, groups, HEAD)
    cached_v = cached_value_rows.reshape(rows_here, length, groups, HEAD)
    recent_k = fresh_keys.reshape(rows_here, -1, groups, HEAD)
    recent_v = fresh_values.reshape(rows_here, -1, groups, HEAD)
    scores = jnp.einsum(
        "rgqd,rlgd->rgql", query, cached_k, preferred_element_type=jnp.float32
    ) / math.sqrt(HEAD)
    fresh_scores = jnp.einsum(
        "rgqd,rlgd->rgql", query, recent_k, preferred_element_type=jnp.float32
    ) / math.sqrt(HEAD)
    weights = jnp.where(valid[:, None, None, :], jnp.exp(scores), jnp.float32(0.0))
    fresh_weights = jnp.exp(fresh_scores)
    total = jnp.sum(weights, axis=-1, keepdims=True) + jnp.sum(
        fresh_weights, axis=-1, keepdims=True
    )
    shares = (weights / total).astype(jnp.bfloat16)
    fresh_shares = (fresh_weights / total).astype(jnp.bfloat16)
    mixed = jnp.einsum("rgql,rlgd->rgqd", shares, cached_v, preferred_element_type=jnp.float32)
    mixed = mixed + jnp.einsum(
        "rgql,rlgd->rgqd", fresh_shares, recent_v, preferred_element_type=jnp.float32
    )
    return mixed.reshape(rows_here, -1).astype(jnp.bfloat16)


def per_device(
    decode_input_rows,
    cached_rotated_keys,
    cached_value_rows,
    lengths,
    base_query_weight,
    base_key_weight,
    base_value_weight,
    base_output_weight,
    query_adapter_down,
    query_adapter_up,
    key_adapter_down,
    key_adapter_up,
    value_adapter_down,
    value_adapter_up,
    output_adapter_down,
    output_adapter_up,
):
    expanded_query_down, expanded_key_down, expanded_value_down, complete_output_rows = (
        lax.all_gather(query_adapter_down, "fsdp", axis=0, tiled=True),
        lax.all_gather(key_adapter_down, "fsdp", axis=0, tiled=True),
        lax.all_gather(value_adapter_down, "fsdp", axis=0, tiled=True),
        lax.all_gather(output_adapter_up, "fsdp", axis=0, tiled=True),
    )
    combined_query_weight = combined_weight_matrix(
        base_query_weight, expanded_query_down, query_adapter_up
    )
    combined_key_weight = combined_weight_matrix(base_key_weight, expanded_key_down, key_adapter_up)
    combined_value_weight = combined_weight_matrix(
        base_value_weight, expanded_value_down, value_adapter_up
    )
    combined_output_weight = combined_weight_matrix(
        base_output_weight, output_adapter_down, complete_output_rows
    )
    rows_here = decode_input_rows.shape[0]
    valid = jnp.arange(cached_rotated_keys.shape[1], dtype=jnp.int32)[None, :] < lengths[:, None]
    fresh_keys = []
    fresh_values = []
    results = []
    for step in range(STEPS):
        stream = decode_input_rows[:, step].astype(jnp.float32)
        if step > 0:
            stream = stream + results[-1].astype(jnp.float32)
        normed = rms_rows(stream).astype(jnp.bfloat16)
        gathered = lax.all_gather(normed, "fsdp", axis=0, tiled=True)
        query = jnp.dot(gathered, combined_query_weight, preferred_element_type=jnp.float32).astype(
            jnp.bfloat16
        )
        key = jnp.dot(gathered, combined_key_weight, preferred_element_type=jnp.float32).astype(
            jnp.bfloat16
        )
        value = jnp.dot(gathered, combined_value_weight, preferred_element_type=jnp.float32).astype(
            jnp.bfloat16
        )
        query, key, value = (
            lax.all_to_all(query, "fsdp", split_axis=0, concat_axis=1, tiled=True),
            lax.all_to_all(key, "fsdp", split_axis=0, concat_axis=1, tiled=True),
            lax.all_to_all(value, "fsdp", split_axis=0, concat_axis=1, tiled=True),
        )
        positions = lengths + step
        query_rot = rotary(rms_rows(query.reshape(rows_here, QHEADS, HEAD)), positions).astype(
            jnp.bfloat16
        )
        key_rot = rotary(rms_rows(key.reshape(rows_here, KVHEADS, HEAD)), positions).astype(
            jnp.bfloat16
        )
        fresh_keys.append(key_rot.reshape(rows_here, -1))
        fresh_values.append(value)
        mixed = attend(
            query_rot,
            cached_rotated_keys,
            cached_value_rows,
            valid,
            jnp.stack(fresh_keys, axis=1),
            jnp.stack(fresh_values, axis=1),
        )
        spread = lax.all_to_all(mixed, "fsdp", split_axis=1, concat_axis=0, tiled=True)
        result = lax.psum_scatter(
            jnp.dot(spread, combined_output_weight, preferred_element_type=jnp.float32),
            "fsdp",
            scatter_dimension=0,
            tiled=True,
        )
        results.append(result.astype(jnp.bfloat16))
    return (
        jnp.stack(results, axis=1),
        jnp.stack(fresh_keys, axis=1),
        jnp.stack(fresh_values, axis=1),
    )


def solution(mesh):
    placed = (
        P(("job", "fsdp"), None, None),
        P(("job", "fsdp"), None, None),
        P(("job", "fsdp"), None, None),
        P(("job", "fsdp")),
        P(None, "fsdp"),
        P(None, "fsdp"),
        P(None, "fsdp"),
        P("fsdp", None),
        P(("job", "fsdp"), None),
        P(("job", "fsdp"), None),
        P(("job", "fsdp"), None),
        P(("job", "fsdp"), None),
        P(("job", "fsdp"), None),
        P(("job", "fsdp"), None),
        P(("job", "fsdp"), None),
        P(("job", "fsdp"), None),
    )
    return jax.shard_map(
        per_device,
        mesh=mesh,
        in_specs=placed,
        out_specs=(
            P(("job", "fsdp"), None, None),
            P(("job", "fsdp"), None, None),
            P(("job", "fsdp"), None, None),
        ),
        check_vma=False,
    )
```

profile of v0, /device:TPU:0, one launch (start us, length us, event | category | flops | bytes accessed | tf_op | source)
XLA Modules:
  0.0 384.3 jit_solution(12682575856774196133)
XLA Ops:
  3.5 24.0 %all-gather = bf16[16,1,5120]{2,1,0:T(2,128)(2,1)S(1)} all-gather(bf16[1,1,5120]{2,1,0:T(2,128)(2,1)S(1)} %multiply_convert_fusion), channel_id=2, replica_groups=mesh['job'=2,'fsdp'=16] {'fsdp'}, dimensions={0}, use_global_device_ids=true | all-gather | bytes 174080 | tf_op jit(solution)/shard_map/all_gather | solution.py:114
  27.5 20.0 %all-gather.3 = bf16[16,320,64]{1,2,0:T(8,128)(2,1)S(1)} all-gather(bf16[1,320,64]{1,2,0:T(8,128)(2,1)} %bitcast.143), channel_id=1, replica_groups=mesh['job'=2,'fsdp'=16] {'fsdp'}, dimensions={0}, use_global_device_ids=true | all-gather | bytes 696320 | tf_op jit(solution)/shard_map/all_gather | solution.py:91
  54.4 24.0 %all-gather.2 = bf16[16,320,64]{1,2,0:T(8,128)(2,1)S(1)} all-gather(bf16[1,320,64]{1,2,0:T(8,128)(2,1)S(1)} %bitcast.144), channel_id=1, replica_groups=mesh['job'=2,'fsdp'=16] {'fsdp'}, dimensions={0}, use_global_device_ids=true | all-gather | bytes 696320 | tf_op jit(solution)/shard_map/all_gather | solution.py:90
  80.8 19.6 %all-gather.1 = bf16[16,320,64]{1,2,0:T(8,128)(2,1)S(1)} all-gather(bf16[1,320,64]{1,2,0:T(8,128)(2,1)S(1)} %bitcast.145), channel_id=1, replica_groups=mesh['job'=2,'fsdp'=16] {'fsdp'}, dimensions={0}, use_global_device_ids=true | all-gather | bytes 696320 | tf_op jit(solution)/shard_map/all_gather | solution.py:89
  101.5 4.0 %add_convert_fusion.1 = bf16[5120,512]{1,0:T(8,128)(2,1)S(1)} fusion(bf16[5120,512]{1,0:T(8,128)(2,1)} %param.20, bf16[5120,64]{0,1:T(8,128)(2,1)S(1)} %reshape.680, bf16[512,64]{0,1:T(8,128)(2,1)S(1)} %copy-done), kind=kOutput, calls=%fused_computation.1 | convolution fusion | flops 346030080 | bytes 11206656 | tf_op jit(solution)/shard_map/dot_general | solution.py:20
  108.7 21.1 %all-gather.4 = bf16[16,320,64]{1,2,0:T(8,128)(2,1)S(1)} all-gather(bf16[1,320,64]{1,2,0:T(8,128)(2,1)S(1)} %bitcast.146), channel_id=1, replica_groups=mesh['job'=2,'fsdp'=16] {'fsdp'}, dimensions={0}, use_global_device_ids=true | all-gather | bytes 696320 | tf_op jit(solution)/shard_map/all_gather | solution.py:92
  130.9 6.3 %add_convert_fusion = bf16[512,5120]{1,0:T(8,128)(2,1)} fusion(bf16[512,5120]{1,0:T(8,128)(2,1)} %param.23, bf16[512,64]{0,1:T(8,128)(2,1)S(1)} %copy-done.5, bf16[5120,64]{0,1:T(8,128)(2,1)S(1)} %reshape.686), kind=kOutput, calls=%fused_computation | convolution fusion | flops 346030080 | bytes 11206656 | tf_op jit(solution)/shard_map/dot_general | solution.py:20
  137.9 3.6 all-to-all-start.1
  143.4 5.4 %copy.82 = bf16[256,8,8,128]{3,2,1,0:T(8,128)(2,1)} copy(bf16[256,8,8,128]{3,1,2,0:T(8,128)(2,1)} %bitcast.131) | data formatting | bytes 8388608
  152.6 5.8 %all-to-all-start = ((bf16[16,2,256]{2,1,0:T(2,128)(2,1)}), bf16[16,2,256]{2,1,0:T(2,128)(2,1)S(1)}, u32[]{:S(2)}, u32[]{:S(2)}) async-start(bf16[16,2,256]{2,1,0:T(2,128)(2,1)} %reshape.714), calls=%async_computation | async-start | bytes 32768 | tf_op jit(solution)/shard_map/all_to_all | solution.py:125
  159.3 5.6 %all-to-all-done = bf16[16,2,256]{2,1,0:T(2,128)(2,1)S(1)} async-done(((bf16[16,2,256]{2,1,0:T(2,128)(2,1)}), bf16[16,2,256]{2,1,0:T(2,128)(2,1)S(1)}, u32[]{:S(2)}, u32[]{:S(2)}) %all-to-all-start) | async-done | bytes 16416 | tf_op jit(solution)/shard_map/all_to_all | solution.py:125
  165.5 3.5 fusion.94
  173.8 3.5 all-to-all-start.3
  177.6 6.2 %all-to-all-done.3 = bf16[16,2,256]{2,1,0:T(2,128)(2,1)S(1)} async-done(((bf16[16,2,256]{2,1,0:T(2,128)(2,1)}), bf16[16,2,256]{2,1,0:T(2,128)(2,1)S(1)}, u32[]{:S(2)}, u32[]{:S(2)}) %all-to-all-start.3) | async-done | bytes 16416 | tf_op jit(solution)/shard_map/all_to_all | solution.py:146
  187.0 60.7 %all-reduce.4 = bf16[16,5120]{1,0:T(8,128)(2,1)S(1)} all-reduce(f32[16,5120]{1,0:T(8,128)S(1)} %fusion.62), channel_id=3, replica_groups=mesh['job'=2,'fsdp'=16] {'fsdp'}, use_global_device_ids=true, to_apply=%region_5.6.clone | all-reduce | flops 81920 | bytes 491520
  250.4 18.0 %all-gather.5 = bf16[16,1,5120]{2,1,0:T(2,128)(2,1)S(1)} all-gather(bf16[1,1,5120]{2,1,0:T(2,128)(2,1)S(1)} %convert_bitcast_fusion), channel_id=1, replica_groups=mesh['job'=2,'fsdp'=16] {'fsdp'}, dimensions={0}, use_global_device_ids=true | all-gather | bytes 174080 | tf_op jit(solution)/shard_map/all_gather | solution.py:114
  269.4 3.6 all-to-all-start.6
  273.8 5.4 %all-to-all-done.6 = bf16[16,1,64]{2,1,0:T(2,128)(2,1)S(1)} async-done(((bf16[16,1,64]{2,1,0:T(2,128)(2,1)}), bf16[16,1,64]{2,1,0:T(2,128)(2,1)S(1)}, u32[]{:S(2)}, u32[]{:S(2)}) %all-to-all-start.6) | async-done | bytes 2080 | tf_op jit(solution)/shard_map/all_to_all | solution.py:127
  289.1 4.3 %all-to-all-start.4 = ((bf16[16,2,256]{2,1,0:T(2,128)(2,1)}), bf16[16,2,256]{2,1,0:T(2,128)(2,1)S(1)}, u32[]{:S(2)}, u32[]{:S(2)}) async-start(bf16[16,2,256]{2,1,0:T(2,128)(2,1)} %reshape.718), calls=%async_computation.4 | async-start | bytes 32768 | tf_op jit(solution)/shard_map/all_to_all | solution.py:125
  294.9 5.0 %all-to-all-done.4 = bf16[16,2,256]{2,1,0:T(2,128)(2,1)S(1)} async-done(((bf16[16,2,256]{2,1,0:T(2,128)(2,1)}), bf16[16,2,256]{2,1,0:T(2,128)(2,1)S(1)}, u32[]{:S(2)}, u32[]{:S(2)}) %all-to-all-start.4) | async-done | bytes 16416 | tf_op jit(solution)/shard_map/all_to_all | solution.py:125
  300.3 3.5 fusion.95
  309.0 3.5 all-to-all-start.7
  313.1 5.9 %all-to-all-done.7 = bf16[16,2,256]{2,1,0:T(2,128)(2,1)S(1)} async-done(((bf16[16,2,256]{2,1,0:T(2,128)(2,1)}), bf16[16,2,256]{2,1,0:T(2,128)(2,1)S(1)}, u32[]{:S(2)}, u32[]{:S(2)}) %all-to-all-start.7) | async-done | bytes 16416 | tf_op jit(solution)/shard_map/all_to_all | solution.py:146
  322.2 60.7 %all-reduce.5 = bf16[16,5120]{1,0:T(8,128)(2,1)S(1)} all-reduce(f32[16,5120]{1,0:T(8,128)S(1)} %fusion.59), channel_id=4, replica_groups=mesh['job'=2,'fsdp'=16] {'fsdp'}, use_global_device_ids=true, to_apply=%region_12.13.clone | all-reduce | flops 81920 | bytes 491520
  (125 shorter events, 57.8 us)
Async XLA Ops:
  0.6 100.9 %copy-start = (bf16[512,64]{0,1:T(8,128)(2,1)S(1)}, bf16[512,64]{0,1:T(8,128)(2,1)}, u32[]{:S(2)}) copy-start(bf16[512,64]{0,1:T(8,128)(2,1)} %param.25) | copy-start | bytes 196612
  0.6 53.7 %copy-start.6 = (bf16[320,64]{0,1:T(8,128)(2,1)S(1)}, bf16[320,64]{0,1:T(8,128)(2,1)}, u32[]{:S(2)}) copy-start(bf16[320,64]{0,1:T(8,128)(2,1)} %param.26) | copy-start | bytes 122884
  27.5 52.0 %copy-start.3 = (bf16[5120,64]{0,1:T(8,128)(2,1)S(1)}, bf16[5120,64]{0,1:T(8,128)(2,1)}, u32[]{:S(2)}) copy-start(bf16[5120,64]{0,1:T(8,128)(2,1)} %param.21) | copy-start | bytes 1966084
  27.5 52.0 %copy-start.9 = (bf16[64,64]{1,0:T(8,128)(2,1)S(1)}, bf16[64,64]{1,0:T(8,128)(2,1)}, u32[]{:S(2)}) copy-start(bf16[64,64]{1,0:T(8,128)(2,1)} %param.27) | copy-start | bytes 24580
  47.9 32.9 %copy-start.7 = (bf16[320,64]{0,1:T(8,128)(2,1)S(1)}, bf16[320,64]{0,1:T(8,128)(2,1)}, u32[]{:S(2)}) copy-start(bf16[320,64]{0,1:T(8,128)(2,1)} %param.24) | copy-start | bytes 122884
  50.9 87.0 %all-to-all-start.2 = ((bf16[16,1,64]{2,1,0:T(2,128)(2,1)}), bf16[16,1,64]{2,1,0:T(2,128)(2,1)S(1)}, u32[]{:S(2)}, u32[]{:S(2)}) async-start(bf16[16,1,64]{2,1,0:T(2,128)(2,1)} %copy.63), calls=%async_computation.2 | async-start | bytes 16384 | tf_op jit(solution)/shard_map/all_to_all | solution.py:127
  105.5 2.3 copy-start.1
  107.9 0.8 copy-start.8
  107.9 23.0 %copy-start.5 = (bf16[512,64]{0,1:T(8,128)(2,1)S(1)}, bf16[512,64]{0,1:T(8,128)(2,1)}, u32[]{:S(2)}) copy-start(bf16[512,64]{0,1:T(8,128)(2,1)} %param.30) | copy-start | bytes 196612
  137.9 14.7 %all-to-all-start.1 = ((bf16[16,1,64]{2,1,0:T(2,128)(2,1)}), bf16[16,1,64]{2,1,0:T(2,128)(2,1)S(1)}, u32[]{:S(2)}, u32[]{:S(2)}) async-start(bf16[16,1,64]{2,1,0:T(2,128)(2,1)} %copy.60), calls=%async_computation.1 | async-start | bytes 16384 | tf_op jit(solution)/shard_map/all_to_all | solution.py:126
  143.4 5.4 %copy-start.2 = (bf16[1,2048,1024]{2,1,0:T(8,128)(2,1)S(1)}, bf16[1,2048,1024]{2,1,0:T(8,128)(2,1)}, u32[]{:S(2)}) copy-start(bf16[1,2048,1024]{2,1,0:T(8,128)(2,1)} %param.18) | copy-start | bytes 12582916
  148.9 3.2 copy-start.10
  152.6 12.3 %all-to-all-start = ((bf16[16,2,256]{2,1,0:T(2,128)(2,1)}), bf16[16,2,256]{2,1,0:T(2,128)(2,1)S(1)}, u32[]{:S(2)}, u32[]{:S(2)}) async-start(bf16[16,2,256]{2,1,0:T(2,128)(2,1)} %reshape.714), calls=%async_computation | async-start | bytes 32768 | tf_op jit(solution)/shard_map/all_to_all | solution.py:125
  172.4 75.4 %copy-start.4 = (bf16[1,2,5120]{2,1,0:T(2,128)(2,1)S(1)}, bf16[1,2,5120]{2,1,0:T(2,128)(2,1)}, u32[]{:S(2)}) copy-start(bf16[1,2,5120]{2,1,0:T(2,128)(2,1)} %param.16) | copy-start | bytes 61444
  173.8 10.0 %all-to-all-start.3 = ((bf16[16,2,256]{2,1,0:T(2,128)(2,1)}), bf16[16,2,256]{2,1,0:T(2,128)(2,1)S(1)}, u32[]{:S(2)}, u32[]{:S(2)}) async-start(bf16[16,2,256]{2,1,0:T(2,128)(2,1)} %reshape.716), calls=%async_computation.3 | async-start | bytes 32768 | tf_op jit(solution)/shard_map/all_to_all | solution.py:146
  269.4 9.9 %all-to-all-start.6 = ((bf16[16,1,64]{2,1,0:T(2,128)(2,1)}), bf16[16,1,64]{2,1,0:T(2,128)(2,1)S(1)}, u32[]{:S(2)}, u32[]{:S(2)}) async-start(bf16[16,1,64]{2,1,0:T(2,128)(2,1)} %copy.72), calls=%async_computation.6 | async-start | bytes 16384 | tf_op jit(solution)/shard_map/all_to_all | solution.py:127
  279.3 9.8 %all-to-all-start.5 = ((bf16[16,1,64]{2,1,0:T(2,128)(2,1)}), bf16[16,1,64]{2,1,0:T(2,128)(2,1)S(1)}, u32[]{:S(2)}, u32[]{:S(2)}) async-start(bf16[16,1,64]{2,1,0:T(2,128)(2,1)} %copy.68), calls=%async_computation.5 | async-start | bytes 16384 | tf_op jit(solution)/shard_map/all_to_all | solution.py:126
  289.1 10.8 %all-to-all-start.4 = ((bf16[16,2,256]{2,1,0:T(2,128)(2,1)}), bf16[16,2,256]{2,1,0:T(2,128)(2,1)S(1)}, u32[]{:S(2)}, u32[]{:S(2)}) async-start(bf16[16,2,256]{2,1,0:T(2,128)(2,1)} %reshape.718), calls=%async_computation.4 | async-start | bytes 32768 | tf_op jit(solution)/shard_map/all_to_all | solution.py:125
  309.0 10.0 %all-to-all-start.7 = ((bf16[16,2,256]{2,1,0:T(2,128)(2,1)}), bf16[16,2,256]{2,1,0:T(2,128)(2,1)S(1)}, u32[]{:S(2)}, u32[]{:S(2)}) async-start(bf16[16,2,256]{2,1,0:T(2,128)(2,1)} %reshape.720), calls=%async_computation.7 | async-start | bytes 32768 | tf_op jit(solution)/shard_map/all_to_all | solution.py:146
where the time goes:
time: 386 us; the launch traced here: 384 us
  blocking collectives  248 us (64%)
  matrix products  38.2 us (10%)
  starting transfers between devices  31.2 us (8%)
  waiting for transfers between devices  29.8 us (8%)
  local copies, waits for them, and re-layouts  23.5 us (6%)
  other arithmetic  10.3 us (3%)
    unnamed x2, blocking collectives  121 us
    all_gather x2, blocking collectives, per_device(): gathered = lax.all_gather(normed, 'fsdp', axis=0, tiled=True)  42 us
    all_gather x1, blocking collectives, per_device(): lax.all_gather(key_adapter_down, 'fsdp', axis=0, tiled=True)  24 us
    all_gather x1, blocking collectives, per_device(): lax.all_gather(output_adapter_up, 'fsdp', axis=0, tiled=True)  21.1 us
    all_gather x1, blocking collectives, per_device(): lax.all_gather(value_adapter_down, 'fsdp', axis=0, tiled=True)  20 us
    all_gather x1, blocking collectives, per_device(): lax.all_gather(query_adapter_down, 'fsdp', axis=0, tiled=True)  19.6 us
    unnamed x37, local copies, waits for them, and re-layouts  16.6 us
    dot_general x4, matrix products, combined_weight_matrix(): delta = jnp.dot(left, right.T, preferred_element_type=jnp.float32)  12.1 us
  transfers between devices with their start and end apart: 8, of which 6 were waited for; matrix products, arithmetic and copies ran while one was open for 9% of the time, Pallas kernels for 0%

commit v1 on v0

--- a/solution.py
+++ b/solution.py
@@ -1,8 +1,11 @@
+import functools
 import math
 
 import jax
 import jax.numpy as jnp
 from jax import lax
+from jax.experimental import pallas as pl
+from jax.experimental.pallas import tpu as pltpu
 from jax.sharding import PartitionSpec as P
 
 QHEADS = 64
@@ -67,7 +70,7 @@
     return mixed.reshape(rows_here, -1).astype(jnp.bfloat16)
 
 
-def per_device(
+def per_device_plain(
     decode_input_rows,
     cached_rotated_keys,
     cached_value_rows,
@@ -158,6 +161,459 @@
     )
 
 
+SLOT = 8
+PIECES = 16
+
+
+def decode_kernel(
+    n,
+    length_ref,
+    x_ref,
+    trig_ref,
+    keys_hbm,
+    values_hbm,
+    wq_hbm,
+    wk_hbm,
+    wv_hbm,
+    wo_hbm,
+    dq_ref,
+    dk_ref,
+    dv_ref,
+    uq_ref,
+    uk_ref,
+    uv_ref,
+    do_ref,
+    uo_ref,
+    out_ref,
+    newk_ref,
+    newv_ref,
+    keys,
+    values,
+    wq,
+    wk,
+    wv,
+    wo,
+    row_send,
+    rows_got,
+    wide,
+    xmat,
+    low_send,
+    low_got,
+    head_send,
+    head_got,
+    mix_send,
+    mix_got,
+    mid_send,
+    mid_got,
+    part_send,
+    part_got,
+    load_sem,
+    send_sem,
+    recv_sem,
+):
+    me = lax.axis_index("fsdp")
+    chunks = x_ref.shape[1]
+    padded = rows_got.shape[1]
+    depth = xmat.shape[2]
+    share = dq_ref.shape[0]
+    rank = dq_ref.shape[1]
+    half = HEAD // 2
+    own_heads = wq.shape[1] // HEAD
+    length = keys.shape[0]
+    group = QHEADS // KVHEADS
+
+    loads = [
+        pltpu.make_async_copy(source, target, load_sem.at[i])
+        for i, (source, target) in enumerate(
+            (
+                (wq_hbm, wq),
+                (wk_hbm, wk),
+                (wv_hbm, wv),
+                (keys_hbm, keys),
+                (values_hbm, values),
+                (wo_hbm, wo),
+            )
+        )
+    ]
+    for load in loads:
+        load.start()
+
+    barrier = pltpu.get_barrier_semaphore()
+
+    def greet(i, carry):
+        pl.semaphore_signal(
+            barrier,
+            inc=1,
+            device_id={"fsdp": lax.rem(me + i, n)},
+            device_id_type=pl.DeviceIdType.MESH,
+        )
+        return carry
+
+    lax.fori_loop(1, n, greet, 0)
+    head_send[...] = jnp.zeros_like(head_send)
+    mix_send[...] = jnp.zeros_like(mix_send)
+    newk_ref[...] = jnp.zeros_like(newk_ref)
+    newv_ref[...] = jnp.zeros_like(newv_ref)
+    part_got[...] = jnp.zeros_like(part_got)
+    pl.semaphore_wait(barrier, n - 1)
+
+    def exchange(which, source_of, target):
+        def send(i, carry):
+            peer = lax.rem(me + i, n)
+            pltpu.make_async_remote_copy(
+                src_ref=source_of(peer),
+                dst_ref=target.at[me],
+                send_sem=send_sem.at[which],
+                recv_sem=recv_sem.at[which],
+                device_id={"fsdp": peer},
+                device_id_type=pl.DeviceIdType.MESH,
+            ).start()
+            return carry
+
+        lax.fori_loop(1, n, send, 0)
+
+    def arrive(which, target):
+        whole = target.at[pl.ds(0, n - 1)]
+        pltpu.make_async_copy(whole, whole, recv_sem.at[which]).wait()
+        pltpu.make_async_copy(whole, whole, send_sem.at[which]).wait()
+
+    odd = lax.rem(me, 2)
+    first_chunk = 5 * (me // 2) + 2 * odd
+    lane = lax.broadcasted_iota(jnp.int32, (KVHEADS, HEAD), 1)
+
+    def step_body(step, carry):
+        stream = x_ref[step] + jnp.sum(part_got[...].astype(jnp.float32), axis=0)[
+            :chunks
+        ].astype(jnp.bfloat16).astype(jnp.float32)
+        mean = jnp.sum(jnp.sum(stream * stream, axis=1, keepdims=True), axis=0, keepdims=True) / (
+            chunks * HEAD
+        )
+        normed = stream * lax.rsqrt(mean + EPSILON)
+        normed = jnp.concatenate(
+            [normed, jnp.zeros((padded - chunks, HEAD), jnp.float32)], axis=0
+        ).astype(jnp.bfloat16)
+        row_send[...] = normed
+        rows_got[me] = normed
+        exchange(0, lambda peer: row_send, rows_got)
+        arrive(0, rows_got)
+        for r in range(n):
+            wide[pl.ds(r * padded, padded), :] = rows_got[r].astype(jnp.float32)
+        mine = [
+            wide[pl.ds(first_chunk + j, n, stride=padded), :] for j in range(3)
+        ]
+        mine = jnp.concatenate(mine, axis=1)
+        mine = jnp.where(odd == 1, mine[:, half : half + share], mine[:, :share]).astype(
+            jnp.bfloat16
+        )
+        low = [
+            jnp.dot(mine, ref[...], preferred_element_type=jnp.float32)
+            for ref in (dq_ref, dk_ref, dv_ref)
+        ]
+        low = jnp.concatenate(low + [jnp.zeros((n, rank), jnp.float32)], axis=1).astype(
+            jnp.bfloat16
+        )
+        low_send[...] = low
+        low_got[me] = low
+        exchange(1, lambda peer: low_send, low_got)
+        per = depth // HEAD
+        for c in range(chunks):
+            xmat[c // per, :, pl.ds((c % per) * HEAD, HEAD)] = wide[
+                pl.ds(c, n, stride=padded), :
+            ].astype(jnp.bfloat16)
+
+        @pl.when(step == 0)
+        def _():
+            for load in loads[:3]:
+                load.wait()
+
+        def project(i, sums):
+            rows = pl.ds(pl.multiple_of(i * depth, depth), depth)
+            left = xmat[i]
+            return tuple(
+                total + jnp.dot(left, ref[rows, :], preferred_element_type=jnp.float32)
+                for total, ref in zip(sums, (wq, wk, wv))
+            )
+
+        query, key, value = lax.fori_loop(
+            0,
+            xmat.shape[0],
+            project,
+            tuple(jnp.zeros((n, ref.shape[1]), jnp.float32) for ref in (wq, wk, wv)),
+        )
+        arrive(1, low_got)
+        low = jnp.sum(low_got[...].astype(jnp.float32), axis=0).astype(jnp.bfloat16)
+
+        def raised(index, ref):
+            return SCALE * lax.dot_general(
+                low[:, index * rank : (index + 1) * rank],
+                ref[...],
+                (((1,), (1,)), ((), ())),
+                preferred_element_type=jnp.float32,
+            )
+
+        query = query + raised(0, uq_ref)
+        pair = jnp.concatenate([key + raised(1, uk_ref), value + raised(2, uv_ref)], axis=1)
+        for j in range(own_heads):
+            head_send[pl.ds(j, n, stride=SLOT), :] = query[:, j * HEAD : (j + 1) * HEAD]
+        head_send[pl.ds(own_heads, n, stride=SLOT), :] = pair
+        send_slots(0 + 2, head_send, head_got)
+        arrive_slots(2, head_got)
+
+        def rounded(array):
+            return array.astype(jnp.bfloat16).astype(jnp.float32)
+
+        cosine = trig_ref[step, 0:1, :]
+        sine = trig_ref[step, 1:2, :]
+
+        def turned(heads):
+            heads = rounded(heads)
+            heads = heads * lax.rsqrt(
+                jnp.sum(heads * heads, axis=1, keepdims=True) / HEAD + EPSILON
+            )
+            return rounded(heads * cosine + pltpu.roll(heads, half, axis=1) * sine)
+
+        even_rows = head_got[pl.ds(own_heads, KVHEADS, stride=2 * SLOT), :]
+        odd_rows = head_got[pl.ds(own_heads + SLOT, KVHEADS, stride=2 * SLOT), :]
+        fresh_key = turned(jnp.where(lane < half, even_rows, pltpu.roll(odd_rows, half, axis=1)))
+        fresh_value = rounded(
+            jnp.where(lane < half, pltpu.roll(even_rows, half, axis=1), odd_rows)
+        )
+        newk_ref[step] = fresh_key
+        newv_ref[step] = fresh_value
+
+        @pl.when(step == 0)
+        def _():
+            loads[3].wait()
+            loads[4].wait()
+
+        known = lax.broadcasted_iota(jnp.int32, (2 * group, length), 1) < length_ref[0]
+        for g in range(0, KVHEADS, 2):
+            heads = jnp.concatenate(
+                [
+                    head_got[pl.ds((2 * g + d) * SLOT, own_heads), :]
+                    for d in range(4)
+                ],
+                axis=0,
+            )
+            heads = turned(heads)
+            low_part = lax.broadcasted_iota(jnp.int32, heads.shape, 0) < group
+            zero = jnp.zeros_like(heads)
+            spread = jnp.concatenate(
+                [jnp.where(low_part, heads, zero), jnp.where(low_part, zero, heads)], axis=1
+            ).astype(jnp.bfloat16)
+            columns = pl.ds(g * HEAD, 2 * HEAD)
+            scores = lax.dot_general(
+                spread,
+                keys[:, columns],
+                (((1,), (1,)), ((), ())),
+                preferred_element_type=jnp.float32,
+            )
+            weights = jnp.where(known, jnp.exp(scores * (1.0 / math.sqrt(HEAD))), 0.0)
+            total = jnp.sum(weights, axis=1, keepdims=True)
+            mixed = jnp.dot(
+                weights.astype(jnp.bfloat16), values[:, columns], preferred_element_type=jnp.float32
+            )
+            mixed = jnp.where(low_part, mixed[:, :HEAD], mixed[:, HEAD:])
+            for t in range(STEPS):
+                k_t = jnp.where(low_part, newk_ref[t, g : g + 1, :], newk_ref[t, g + 1 : g + 2, :])
+                v_t = jnp.where(low_part, newv_ref[t, g : g + 1, :], newv_ref[t, g + 1 : g + 2, :])
+                fresh = jnp.exp(
+                    jnp.sum(heads * k_t, axis=1, keepdims=True) * (1.0 / math.sqrt(HEAD))
+                )
+                fresh = jnp.where(step >= t, fresh, 0.0)
+                total = total + fresh
+                mixed = mixed + rounded(fresh) * v_t
+            mixed = mixed / total
+            for d in range(4):
+                mix_send[pl.ds((2 * g + d) * SLOT, own_heads), :] = mixed[
+                    d * own_heads : (d + 1) * own_heads
+                ]
+        send_slots(3, mix_send, mix_got)
+        arrive_slots(3, mix_got)
+        mixed = jnp.concatenate(
+            [mix_got[pl.ds(j, n, stride=SLOT), :] for j in range(own_heads)], axis=1
+        ).astype(jnp.bfloat16)
+        mid = jnp.dot(mixed, do_ref[...], preferred_element_type=jnp.float32)
+        mid = jnp.concatenate([mid, jnp.zeros((n, HEAD - rank), jnp.float32)], axis=1).astype(
+            jnp.bfloat16
+        )
+        mid_send[...] = mid
+        mid_got[me] = mid
+        exchange(4, lambda peer: mid_send, mid_got)
+
+        @pl.when(step == 0)
+        def _():
+            loads[5].wait()
+
+        for i in range(chunks // per):
+            piece = jnp.dot(
+                mixed, wo[:, pl.ds(i * depth, depth)], preferred_element_type=jnp.float32
+            )
+            for j in range(per):
+                wide[pl.ds(i * per + j, n, stride=padded), :] = piece[:, j * HEAD : (j + 1) * HEAD]
+        arrive(4, mid_got)
+        mid = jnp.sum(mid_got[...].astype(jnp.float32), axis=0).astype(jnp.bfloat16)
+        extra = SCALE * lax.dot_general(
+            mid[:, :rank], uo_ref[...], (((1,), (1,)), ((), ())), preferred_element_type=jnp.float32
+        )
+        gap = jnp.zeros((n, half), jnp.float32)
+        extra = jnp.where(
+            odd == 1,
+            jnp.concatenate([gap, extra], axis=1),
+            jnp.concatenate([extra, gap], axis=1),
+        )
+        for j in range(3):
+            place = pl.ds(first_chunk + j, n, stride=padded)
+            wide[place, :] = wide[place, :] + extra[:, j * HEAD : (j + 1) * HEAD]
+        for r in range(n):
+            part_send[r] = wide[pl.ds(r * padded, padded), :].astype(jnp.bfloat16)
+        part_got[me] = part_send[me]
+        exchange(5, lambda peer: part_send.at[peer], part_got)
+        arrive(5, part_got)
+        out_ref[step] = jnp.sum(part_got[...].astype(jnp.float32), axis=0)[:chunks]
+        return carry
+
+    def send_slots(which, source, target):
+        target[pl.ds(pl.multiple_of(me * SLOT, SLOT), SLOT), :] = source[
+            pl.ds(pl.multiple_of(me * SLOT, SLOT), SLOT), :
+        ]
+
+        def send(i, carry):
+            peer = lax.rem(me + i, n)
+            pltpu.make_async_remote_copy(
+                src_ref=source.at[pl.ds(pl.multiple_of(peer * SLOT, SLOT), SLOT), :],
+                dst_ref=target.at[pl.ds(pl.multiple_of(me * SLOT, SLOT), SLOT), :],
+                send_sem=send_sem.at[which],
+                recv_sem=recv_sem.at[which],
+                device_id={"fsdp": peer},
+                device_id_type=pl.DeviceIdType.MESH,
+            ).start()
+            return carry
+
+        lax.fori_loop(1, n, send, 0)
+
+    def arrive_slots(which, target):
+        whole = target.at[pl.ds(0, (n - 1) * SLOT), :]
+        pltpu.make_async_copy(whole, whole, recv_sem.at[which]).wait()
+        pltpu.make_async_copy(whole, whole, send_sem.at[which]).wait()
+
+    lax.fori_loop(0, STEPS, step_body, 0)
+
+
+def per_device(n, *arrays):
+    (
+        decode_input_rows,
+        cached_rotated_keys,
+        cached_value_rows,
+        lengths,
+        base_query_weight,
+        base_key_weight,
+        base_value_weight,
+        base_output_weight,
+        query_adapter_down,
+        query_adapter_up,
+        key_adapter_down,
+        key_adapter_up,
+        value_adapter_down,
+        value_adapter_up,
+        output_adapter_down,
+        output_adapter_up,
+    ) = arrays
+    rows_here, steps, width = decode_input_rows.shape
+    fits = (
+        rows_here == 1
+        and n == PIECES
+        and base_query_weight.shape[1] == 4 * HEAD
+        and base_key_weight.shape[1] * 2 == HEAD
+        and query_adapter_down.shape[0] * 2 == 5 * HEAD
+        and output_adapter_up.shape[0] * 2 == 5 * HEAD
+    )
+    if not fits:
+        return per_device_plain(*arrays)
+    chunks = width // HEAD
+    padded = -(-chunks // 16) * 16
+    length, kv_width = cached_rotated_keys.shape[1:]
+    depth = 4 * HEAD
+    rank = query_adapter_down.shape[1]
+    half_size = HEAD // 2
+    frequency = THETA ** (-2.0 * jnp.arange(half_size, dtype=jnp.float32) / HEAD)
+    positions = (lengths[0] + jnp.arange(steps, dtype=jnp.int32)).astype(jnp.float32)
+    angles = positions[:, None] * frequency[None, :]
+    cosine, sine = jnp.cos(angles), jnp.sin(angles)
+    trig = jnp.stack(
+        [
+            jnp.concatenate([cosine, cosine], axis=1),
+            jnp.concatenate([-sine, sine], axis=1),
+        ],
+        axis=1,
+    )
+    vmem = pl.BlockSpec(memory_space=pltpu.VMEM)
+    anywhere = pl.BlockSpec(memory_space=pl.ANY)
+    smem = pl.BlockSpec(memory_space=pltpu.SMEM)
+    bf16, f32 = jnp.bfloat16, jnp.float32
+    out, new_keys, new_values = pl.pallas_call(
+        functools.partial(decode_kernel, n),
+        out_shape=(
+            jax.ShapeDtypeStruct((steps, chunks, HEAD), f32),
+            jax.ShapeDtypeStruct((steps, KVHEADS, HEAD), f32),
+            jax.ShapeDtypeStruct((steps, KVHEADS, HEAD), f32),
+        ),
+        in_specs=[smem, vmem, vmem] + [anywhere] * 6 + [vmem] * 8,
+        out_specs=(vmem, vmem, vmem),
+        scratch_shapes=[
+            pltpu.VMEM((length, kv_width), bf16),
+            pltpu.VMEM((length, kv_width), bf16),
+            pltpu.VMEM(base_query_weight.shape, bf16),
+            pltpu.VMEM(base_key_weight.shape, bf16),
+            pltpu.VMEM(base_value_weight.shape, bf16),
+            pltpu.VMEM(base_output_weight.shape, bf16),
+            pltpu.VMEM((padded, HEAD), bf16),
+            pltpu.VMEM((n, padded, HEAD), bf16),
+            pltpu.VMEM((n * padded, HEAD), f32),
+            pltpu.VMEM((width // depth, n, depth), bf16),
+            pltpu.VMEM((n, 4 * rank), bf16),
+            pltpu.VMEM((n, n, 4 * rank), bf16),
+            pltpu.VMEM((n * SLOT, HEAD), f32),
+            pltpu.VMEM((n * SLOT, HEAD), f32),
+            pltpu.VMEM((n * SLOT, HEAD), f32),
+            pltpu.VMEM((n * SLOT, HEAD), f32),
+            pltpu.VMEM((n, HEAD), bf16),
+            pltpu.VMEM((n, n, HEAD), bf16),
+            pltpu.VMEM((n, padded, HEAD), bf16),
+            pltpu.VMEM((n, padded, HEAD), bf16),
+            pltpu.SemaphoreType.DMA((6,)),
+            pltpu.SemaphoreType.DMA((6,)),
+            pltpu.SemaphoreType.DMA((6,)),
+        ],
+        compiler_params=pltpu.CompilerParams(
+            collective_id=0, has_side_effects=True, vmem_limit_bytes=48 * 1024 * 1024
+        ),
+    )(
+        lengths,
+        decode_input_rows.astype(f32).reshape(steps, chunks, HEAD),
+        trig,
+        cached_rotated_keys.reshape(length, kv_width),
+        cached_value_rows.reshape(length, kv_width),
+        base_query_weight,
+        base_key_weight,
+        base_value_weight,
+        base_output_weight,
+        query_adapter_down,
+        key_adapter_down,
+        value_adapter_down,
+        query_adapter_up,
+        key_adapter_up,
+        value_adapter_up,
+        output_adapter_down,
+        output_adapter_up,
+    )
+    return (
+        out.reshape(1, steps, width).astype(bf16),
+        new_keys.reshape(1, steps, kv_width).astype(bf16),
+        new_values.reshape(1, steps, kv_width).astype(bf16),
+    )
+
+
 def solution(mesh):
     placed = (
         P(("job", "fsdp"), None, None),
@@ -178,7 +634,7 @@
         P(("job", "fsdp"), None),
     )
     return jax.shard_map(
-        per_device,
+        functools.partial(per_device, mesh.shape["fsdp"]),
         mesh=mesh,
         in_specs=placed,
         out_specs=(

time: 386 us -> 84.1 us (0.22)
  blocking collectives: 248 us -> 0 us
  Pallas kernels: 0 us -> 70.4 us
  matrix products: 38.2 us -> 0 us
  starting transfers between devices: 31.2 us -> 0 us
  waiting for transfers between devices: 29.8 us -> 0 us
  local copies, waits for them, and re-layouts: 23.5 us -> 10.7 us
  other arithmetic: 10.3 us -> 0.97 us
    all_gather x6 -> x0, blocking collectives: 127 us -> none  [the longest x2 42 us: per_device(): gathered = lax.all_gather(normed, 'fsdp', axis=0, tiled=True)]
    unnamed x2 -> x0, blocking collectives: 121 us -> none
    pallas_call x0 -> x1, Pallas kernels: none -> 70.4 us  [per_device(): pl.pallas_call(functools.partial(decode_kernel, n), out_shape=(jax.ShapeD...]
    dot_general x19 -> x0, matrix products: 38.2 us -> none  [the longest x4 12.1 us: combined_weight_matrix(): delta = jnp.dot(left, right.T, preferred_element_type=jnp.float32)]
    all_to_all x8 -> x0, starting transfers between devices: 31.2 us -> none  [the longest x2 10.1 us: per_device(): lax.all_to_all(query, 'fsdp', split_axis=0, concat_axis=1, tiled=True)]
    all_to_all x8 -> x0, waiting for transfers between devices: 29.8 us -> none  [the longest x2 12 us: per_device(): lax.all_to_all(mixed, 'fsdp', split_axis=1, concat_axis=0, tiled=True)]
    unnamed x37 -> x13, local copies, waits for them, and re-layouts: 16.6 us -> 8.92 us
  transfers between devices with their start and end apart: 8 -> 0, of which waited for: 6 -> 0; matrix products, arithmetic and copies ran while one was open for 9% -> 0% of each run, Pallas kernels for 0% -> 0%
where the time goes in v1:
time: 84.1 us; the launch traced here: 83.5 us
  Pallas kernels  70.4 us (84%)
  local copies, waits for them, and re-layouts  10.7 us (13%)
  between operations  1.41 us (2%)
  other arithmetic  0.97 us (1%)
    pallas_call x1, Pallas kernels, per_device(): pl.pallas_call(functools.partial(decode_kernel, n), out_shape=(jax.ShapeD...  70.4 us
    unnamed x13, local copies, waits for them, and re-layouts  8.92 us

profile of v1, /device:TPU:0, one launch (start us, length us, event | category | flops | bytes accessed | tf_op | source)
XLA Modules:
  0.0 83.5 jit_solution(15294040449281054957)
XLA Ops:
  0.6 0.0 copy-start.1
  0.6 0.0 copy-start
  1.3 0.1 multiply_cosine_fusion
  1.4 0.1 pad_maximum_fusion.1
  1.5 0.7 convert_bitcast_fusion
  2.3 0.9 %copy.22.dq_ref = bf16[320,64]{1,0:T(8,128)(2,1)S(1)} copy(bf16[320,64]{0,1:T(8,128)(2,1)} %param.24) | data formatting | bytes 81920 | tf_op args[8]
  3.2 0.9 %copy.23.dk_ref = bf16[320,64]{1,0:T(8,128)(2,1)S(1)} copy(bf16[320,64]{0,1:T(8,128)(2,1)} %param.26) | data formatting | bytes 81920 | tf_op args[10]
  4.1 0.9 %copy.24.dv_ref = bf16[320,64]{1,0:T(8,128)(2,1)S(1)} copy(bf16[320,64]{0,1:T(8,128)(2,1)} %param.28) | data formatting | bytes 81920 | tf_op args[12]
  5.1 0.9 %copy.27.uo_ref = bf16[320,64]{1,0:T(8,128)(2,1)S(1)} copy(bf16[320,64]{0,1:T(8,128)(2,1)} %param.31) | data formatting | bytes 81920 | tf_op args[15]
  6.0 1.0 %copy.25.uq_ref = bf16[512,64]{1,0:T(8,128)(2,1)S(1)} copy(bf16[512,64]{0,1:T(8,128)(2,1)} %param.25) | data formatting | bytes 131072 | tf_op args[9]
  6.9 1.0 %copy.26.do_ref = bf16[512,64]{1,0:T(8,128)(2,1)S(1)} copy(bf16[512,64]{0,1:T(8,128)(2,1)} %param.30) | data formatting | bytes 131072 | tf_op args[14]
  7.9 1.7 %copy.20.wk_hbm = bf16[5120,64]{1,0:T(8,128)(2,1)S(1)} copy(bf16[5120,64]{0,1:T(8,128)(2,1)} %param.21) | data formatting | bytes 1310720 | tf_op args[5]
  9.6 1.7 %copy.21.wv_hbm = bf16[5120,64]{1,0:T(8,128)(2,1)S(1)} copy(bf16[5120,64]{0,1:T(8,128)(2,1)} %param.22) | data formatting | bytes 1310720 | tf_op args[6]
  11.2 0.0 copy-done.1
  11.3 0.0 copy-done
  11.3 70.4 %shard_map.175 = (f32[2,40,128]{2,1,0:T(8,128)S(1)}, f32[2,8,128]{2,1,0:T(8,128)S(1)}, f32[2,8,128]{2,1,0:T(8,128)S(1)}) custom-call(s32[1]{0:T(128)} %copy.31.length_ref, f32[2,40,128]{2,1,0:T(8,128)S(1)} %bitcast.14, f32[2,2,128]{2,1,0:T(2,128)S(1)} %pad_maximum_fusion.trig_ref, bf16[2048,1024]{1,0:T(8,128)(2,1)} %bitcast.15, bf16[2048,1024]{1,0:T(8,128)(2,1)} %bitcast.16, ...), custom_call_target="tpu_custom_call" | custom-call | tf_op jit(solution)/shard_map/pallas_call | solution.py:554
  81.7 0.6 convert_element_type.52
  82.3 0.6 convert_element_type.54
  82.9 0.6 convert_element_type.56
  (7 shorter events, 0.0 us)
Async XLA Ops:
  0.6 10.6 %copy-start.1 = (bf16[64,64]{1,0:T(8,128)(2,1)S(1)}, bf16[64,64]{1,0:T(8,128)(2,1)}, u32[]{:S(2)}) copy-start(bf16[64,64]{1,0:T(8,128)(2,1)} %uv_ref.1) | copy-start | bytes 24580
  0.6 10.6 %copy-start = (bf16[64,64]{1,0:T(8,128)(2,1)S(1)}, bf16[64,64]{1,0:T(8,128)(2,1)}, u32[]{:S(2)}) copy-start(bf16[64,64]{1,0:T(8,128)(2,1)} %uk_ref.1) | copy-start | bytes 24580

commit v2 on v1

--- a/solution.py
+++ b/solution.py
@@ -176,47 +176,48 @@
     wk_hbm,
     wv_hbm,
     wo_hbm,
-    dq_ref,
-    dk_ref,
-    dv_ref,
-    uq_ref,
-    uk_ref,
-    uv_ref,
-    do_ref,
-    uo_ref,
+    dq_hbm,
+    dk_hbm,
+    dv_hbm,
+    uq_hbm,
+    uk_hbm,
+    uv_hbm,
+    do_hbm,
+    uo_hbm,
     out_ref,
     newk_ref,
     newv_ref,
     keys,
     values,
     wq,
-    wk,
-    wv,
+    wkv,
     wo,
-    row_send,
-    rows_got,
-    wide,
-    xmat,
-    low_send,
-    low_got,
+    down,
+    up_q,
+    up_kv,
+    down_o,
+    up_o,
+    rows_in,
+    in_send,
+    in_got,
+    cols_send,
+    cols_got,
     head_send,
     head_got,
     mix_send,
     mix_got,
-    mid_send,
-    mid_got,
     part_send,
     part_got,
+    block_cols,
+    last_send,
+    last_got,
     load_sem,
     send_sem,
     recv_sem,
 ):
     me = lax.axis_index("fsdp")
-    chunks = x_ref.shape[1]
-    padded = rows_got.shape[1]
-    depth = xmat.shape[2]
-    share = dq_ref.shape[0]
-    rank = dq_ref.shape[1]
+    chunks = x_ref.shape[2] // HEAD
+    rank, share = dq_hbm.shape
     half = HEAD // 2
     own_heads = wq.shape[1] // HEAD
     length = keys.shape[0]
@@ -226,11 +227,19 @@
         pltpu.make_async_copy(source, target, load_sem.at[i])
         for i, (source, target) in enumerate(
             (
+                (dq_hbm, down.at[pl.ds(0, rank), :]),
+                (dk_hbm, down.at[pl.ds(rank, rank), :]),
+                (dv_hbm, down.at[pl.ds(2 * rank, rank), :]),
                 (wq_hbm, wq),
-                (wk_hbm, wk),
-                (wv_hbm, wv),
+                (wk_hbm, wkv.at[pl.ds(0, half), :]),
+                (wv_hbm, wkv.at[pl.ds(half, half), :]),
+                (uq_hbm, up_q),
+                (uk_hbm, up_kv.at[0]),
+                (uv_hbm, up_kv.at[1]),
                 (keys_hbm, keys),
                 (values_hbm, values),
+                (do_hbm, down_o),
+                (uo_hbm, up_o),
                 (wo_hbm, wo),
             )
         )
@@ -250,11 +259,23 @@
         return carry
 
     lax.fori_loop(1, n, greet, 0)
+    for c in range(chunks):
+        rows_in[pl.ds(c, STEPS, stride=chunks), :] = x_ref[
+            0, :, c * HEAD : (c + 1) * HEAD
+        ].astype(jnp.float32)
     head_send[...] = jnp.zeros_like(head_send)
+    down[pl.ds(3 * rank, rank), :] = jnp.zeros((rank, share), jnp.bfloat16)
     mix_send[...] = jnp.zeros_like(mix_send)
     newk_ref[...] = jnp.zeros_like(newk_ref)
     newv_ref[...] = jnp.zeros_like(newv_ref)
-    part_got[...] = jnp.zeros_like(part_got)
+    in_send[...] = jnp.zeros_like(in_send)
+    last_send[...] = jnp.zeros_like(last_send)
+    block_cols[...] = jnp.zeros_like(block_cols)
+    out_ref[...] = jnp.zeros_like(out_ref)
+    firsts = [5 * (d // 2) + 2 * (d % 2) for d in range(n)]
+    for d, first in enumerate(firsts):
+        for t in range(STEPS):
+            in_send[pl.ds(d * SLOT + 3 * t, 3), :] = rows_in[pl.ds(t * chunks + first, 3), :]
     pl.semaphore_wait(barrier, n - 1)
 
     def exchange(which, source_of, target):
@@ -278,81 +299,73 @@
         pltpu.make_async_copy(whole, whole, send_sem.at[which]).wait()
 
     odd = lax.rem(me, 2)
-    first_chunk = 5 * (me // 2) + 2 * odd
     lane = lax.broadcasted_iota(jnp.int32, (KVHEADS, HEAD), 1)
 
     def step_body(step, carry):
-        stream = x_ref[step] + jnp.sum(part_got[...].astype(jnp.float32), axis=0)[
-            :chunks
-        ].astype(jnp.bfloat16).astype(jnp.float32)
-        mean = jnp.sum(jnp.sum(stream * stream, axis=1, keepdims=True), axis=0, keepdims=True) / (
-            chunks * HEAD
-        )
-        normed = stream * lax.rsqrt(mean + EPSILON)
-        normed = jnp.concatenate(
-            [normed, jnp.zeros((padded - chunks, HEAD), jnp.float32)], axis=0
-        ).astype(jnp.bfloat16)
-        row_send[...] = normed
-        rows_got[me] = normed
-        exchange(0, lambda peer: row_send, rows_got)
-        arrive(0, rows_got)
-        for r in range(n):
-            wide[pl.ds(r * padded, padded), :] = rows_got[r].astype(jnp.float32)
-        mine = [
-            wide[pl.ds(first_chunk + j, n, stride=padded), :] for j in range(3)
-        ]
+        mine = []
+        for j in range(3):
+            early = in_got[pl.ds(j, n, stride=SLOT), :]
+            late = in_got[pl.ds(3 + j, n, stride=SLOT), :]
+            mine.append(jnp.where(step == 0, early, late))
         mine = jnp.concatenate(mine, axis=1)
-        mine = jnp.where(odd == 1, mine[:, half : half + share], mine[:, :share]).astype(
-            jnp.bfloat16
-        )
-        low = [
-            jnp.dot(mine, ref[...], preferred_element_type=jnp.float32)
-            for ref in (dq_ref, dk_ref, dv_ref)
-        ]
-        low = jnp.concatenate(low + [jnp.zeros((n, rank), jnp.float32)], axis=1).astype(
-            jnp.bfloat16
-        )
-        low_send[...] = low
-        low_got[me] = low
-        exchange(1, lambda peer: low_send, low_got)
-        per = depth // HEAD
-        for c in range(chunks):
-            xmat[c // per, :, pl.ds((c % per) * HEAD, HEAD)] = wide[
-                pl.ds(c, n, stride=padded), :
-            ].astype(jnp.bfloat16)
+        mine = jnp.where(odd == 1, mine[:, half : half + share], mine[:, :share])
+        stream = mine + block_cols[0]
 
         @pl.when(step == 0)
         def _():
             for load in loads[:3]:
                 load.wait()
 
-        def project(i, sums):
-            rows = pl.ds(pl.multiple_of(i * depth, depth), depth)
-            left = xmat[i]
-            return tuple(
-                total + jnp.dot(left, ref[rows, :], preferred_element_type=jnp.float32)
-                for total, ref in zip(sums, (wq, wk, wv))
-            )
-
-        query, key, value = lax.fori_loop(
-            0,
-            xmat.shape[0],
-            project,
-            tuple(jnp.zeros((n, ref.shape[1]), jnp.float32) for ref in (wq, wk, wv)),
-        )
-        arrive(1, low_got)
-        low = jnp.sum(low_got[...].astype(jnp.float32), axis=0).astype(jnp.bfloat16)
-
-        def raised(index, ref):
+        low = lax.dot_general(
+            stream.astype(jnp.bfloat16), down[...], (((1,), (1,)), ((), ())), preferred_element_type=jnp.float32
+        )
+        columns = jnp.concatenate([stream, low[:, : 3 * rank]], axis=1).astype(jnp.bfloat16)
+        cols_send[...] = columns
+        cols_got[me] = columns
+        exchange(1, lambda peer: cols_send, cols_got)
+        arrive(1, cols_got)
+
+        @pl.when(step == 0)
+        def _():
+            for load in loads[3:9]:
+                load.wait()
+
+        query = jnp.zeros((n, wq.shape[1]), jnp.float32)
+        pair = jnp.zeros((n, HEAD), jnp.float32)
+        squares = jnp.zeros((n, 1), jnp.float32)
+        for i in range(n // 2):
+            features = pl.ds(i * 2 * share, 2 * share)
+            left = jnp.concatenate(
+                [
+                    cols_got[2 * i].astype(jnp.float32)[:, :share],
+                    cols_got[2 * i + 1].astype(jnp.float32)[:, :share],
+                ],
+                axis=1,
+            )
+            squares = squares + jnp.sum(left * left, axis=1, keepdims=True)
+            left = left.astype(jnp.bfloat16)
+            query = query + jnp.dot(left, wq[features, :], preferred_element_type=jnp.float32)
+            pair = pair + lax.dot_general(
+                left,
+                wkv[:, features],
+                (((1,), (1,)), ((), ())),
+                preferred_element_type=jnp.float32,
+            )
+        inverse = lax.rsqrt(squares / (chunks * HEAD) + EPSILON)
+        low = jnp.sum(cols_got[...].astype(jnp.float32), axis=0)[:, share:].astype(jnp.bfloat16)
+
+        def raised(index, factor, rank_dim):
             return SCALE * lax.dot_general(
                 low[:, index * rank : (index + 1) * rank],
-                ref[...],
-                (((1,), (1,)), ((), ())),
+                factor,
+                (((1,), (rank_dim,)), ((), ())),
                 preferred_element_type=jnp.float32,
             )
 
-        query = query + raised(0, uq_ref)
-        pair = jnp.concatenate([key + raised(1, uk_ref), value + raised(2, uv_ref)], axis=1)
+        query = inverse * (query + raised(0, up_q[...], 0))
+        pair = inverse * (
+            pair + jnp.concatenate([raised(1, up_kv[0], 1), raised(2, up_kv[1], 1)], axis=1)
+        )
         for j in range(own_heads):
             head_send[pl.ds(j, n, stride=SLOT), :] = query[:, j * HEAD : (j + 1) * HEAD]
         head_send[pl.ds(own_heads, n, stride=SLOT), :] = pair
@@ -383,8 +396,8 @@
 
         @pl.when(step == 0)
         def _():
-            loads[3].wait()
-            loads[4].wait()
+            loads[9].wait()
+            loads[10].wait()
 
         known = lax.broadcasted_iota(jnp.int32, (2 * group, length), 1) < length_ref[0]
         for g in range(0, KVHEADS, 2):
@@ -433,44 +446,43 @@
         mixed = jnp.concatenate(
             [mix_got[pl.ds(j, n, stride=SLOT), :] for j in range(own_heads)], axis=1
         ).astype(jnp.bfloat16)
-        mid = jnp.dot(mixed, do_ref[...], preferred_element_type=jnp.float32)
-        mid = jnp.concatenate([mid, jnp.zeros((n, HEAD - rank), jnp.float32)], axis=1).astype(
-            jnp.bfloat16
-        )
-        mid_send[...] = mid
-        mid_got[me] = mid
-        exchange(4, lambda peer: mid_send, mid_got)
 
         @pl.when(step == 0)
         def _():
-            loads[5].wait()
-
-        for i in range(chunks // per):
+            for load in loads[11:]:
+                load.wait()
+
+        mid = lax.dot_general(
+            mixed, down_o[...], (((1,), (1,)), ((), ())), preferred_element_type=jnp.float32
+        )
+        for i in range(n // 2):
             piece = jnp.dot(
-                mixed, wo[:, pl.ds(i * depth, depth)], preferred_element_type=jnp.float32
-            )
-            for j in range(per):
-                wide[pl.ds(i * per + j, n, stride=padded), :] = piece[:, j * HEAD : (j + 1) * HEAD]
-        arrive(4, mid_got)
-        mid = jnp.sum(mid_got[...].astype(jnp.float32), axis=0).astype(jnp.bfloat16)
-        extra = SCALE * lax.dot_general(
-            mid[:, :rank], uo_ref[...], (((1,), (1,)), ((), ())), preferred_element_type=jnp.float32
-        )
+                mixed, wo[:, pl.ds(i * 2 * share, 2 * share)], preferred_element_type=jnp.float32
+            )
+            part_send[2 * i] = jnp.concatenate([piece[:, :share], mid], axis=1).astype(jnp.bfloat16)
+            part_send[2 * i + 1] = jnp.concatenate([piece[:, share:], mid], axis=1).astype(
+                jnp.bfloat16
+            )
+        part_got[me] = part_send[me]
+        exchange(4, lambda peer: part_send.at[peer], part_got)
+        arrive(4, part_got)
+        summed = jnp.sum(part_got[...].astype(jnp.float32), axis=0)
+        block = rounded(
+            summed[:, :share]
+            + SCALE
+            * jnp.dot(
+                summed[:, share:].astype(jnp.bfloat16), up_o[...], preferred_element_type=jnp.float32
+            )
+        )
+        block_cols[0] = block
         gap = jnp.zeros((n, half), jnp.float32)
-        extra = jnp.where(
+        block = jnp.where(
             odd == 1,
-            jnp.concatenate([gap, extra], axis=1),
-            jnp.concatenate([extra, gap], axis=1),
+            jnp.concatenate([gap, block], axis=1),
+            jnp.concatenate([block, gap], axis=1),
         )
         for j in range(3):
-            place = pl.ds(first_chunk + j, n, stride=padded)
-            wide[place, :] = wide[place, :] + extra[:, j * HEAD : (j + 1) * HEAD]
-        for r in range(n):
-            part_send[r] = wide[pl.ds(r * padded, padded), :].astype(jnp.bfloat16)
-        part_got[me] = part_send[me]
-        exchange(5, lambda peer: part_send.at[peer], part_got)
-        arrive(5, part_got)
-        out_ref[step] = jnp.sum(part_got[...].astype(jnp.float32), axis=0)[:chunks]
+            last_send[pl.ds(3 * step + j, n, stride=SLOT), :] = block[:, j * HEAD : (j + 1) * HEAD]
         return carry
 
     def send_slots(which, source, target):
@@ -497,7 +509,17 @@
         pltpu.make_async_copy(whole, whole, recv_sem.at[which]).wait()
         pltpu.make_async_copy(whole, whole, send_sem.at[which]).wait()
 
+    send_slots(0, in_send, in_got)
+    arrive_slots(0, in_got)
     lax.fori_loop(0, STEPS, step_body, 0)
+    send_slots(5, last_send, last_got)
+    arrive_slots(5, last_got)
+    for d, first in enumerate(firsts):
+        for t in range(STEPS):
+            place = pl.ds(first, 3)
+            out_ref[t, place, :] = (
+                out_ref[t, place, :] + last_got[pl.ds(d * SLOT + 3 * t, 3), :]
+            )
 
 
 def per_device(n, *arrays):
@@ -531,9 +553,7 @@
     if not fits:
         return per_device_plain(*arrays)
     chunks = width // HEAD
-    padded = -(-chunks // 16) * 16
     length, kv_width = cached_rotated_keys.shape[1:]
-    depth = 4 * HEAD
     rank = query_adapter_down.shape[1]
     half_size = HEAD // 2
     frequency = THETA ** (-2.0 * jnp.arange(half_size, dtype=jnp.float32) / HEAD)
@@ -558,54 +578,58 @@
             jax.ShapeDtypeStruct((steps, KVHEADS, HEAD), f32),
             jax.ShapeDtypeStruct((steps, KVHEADS, HEAD), f32),
         ),
-        in_specs=[smem, vmem, vmem] + [anywhere] * 6 + [vmem] * 8,
+        in_specs=[smem, vmem, vmem] + [anywhere] * 14,
         out_specs=(vmem, vmem, vmem),
         scratch_shapes=[
             pltpu.VMEM((length, kv_width), bf16),
             pltpu.VMEM((length, kv_width), bf16),
             pltpu.VMEM(base_query_weight.shape, bf16),
-            pltpu.VMEM(base_key_weight.shape, bf16),
-            pltpu.VMEM(base_value_weight.shape, bf16),
+            pltpu.VMEM((HEAD, width), bf16),
             pltpu.VMEM(base_output_weight.shape, bf16),
-            pltpu.VMEM((padded, HEAD), bf16),
-            pltpu.VMEM((n, padded, HEAD), bf16),
-            pltpu.VMEM((n * padded, HEAD), f32),
-            pltpu.VMEM((width // depth, n, depth), bf16),
-            pltpu.VMEM((n, 4 * rank), bf16),
-            pltpu.VMEM((n, n, 4 * rank), bf16),
-            pltpu.VMEM((n * SLOT, HEAD), f32),
-            pltpu.VMEM((n * SLOT, HEAD), f32),
-            pltpu.VMEM((n * SLOT, HEAD), f32),
-            pltpu.VMEM((n * SLOT, HEAD), f32),
-            pltpu.VMEM((n, HEAD), bf16),
-            pltpu.VMEM((n, n, HEAD), bf16),
-            pltpu.VMEM((n, padded, HEAD), bf16),
-            pltpu.VMEM((n, padded, HEAD), bf16),
-            pltpu.SemaphoreType.DMA((6,)),
+            pltpu.VMEM((4 * rank, width // n), bf16),
+            pltpu.VMEM((rank, base_query_weight.shape[1]), bf16),
+            pltpu.VMEM((2, half_size, rank), bf16),
+            pltpu.VMEM((rank, base_output_weight.shape[0]), bf16),
+            pltpu.VMEM((rank, width // n), bf16),
+            pltpu.VMEM((steps * chunks, HEAD), f32),
+            pltpu.VMEM((n * SLOT, HEAD), f32),
+            pltpu.VMEM((n * SLOT, HEAD), f32),
+            pltpu.VMEM((n, width // n + 3 * rank), bf16),
+            pltpu.VMEM((n, n, width // n + 3 * rank), bf16),
+            pltpu.VMEM((n * SLOT, HEAD), f32),
+            pltpu.VMEM((n * SLOT, HEAD), f32),
+            pltpu.VMEM((n * SLOT, HEAD), f32),
+            pltpu.VMEM((n * SLOT, HEAD), f32),
+            pltpu.VMEM((n, n, width // n + rank), bf16),
+            pltpu.VMEM((n, n, width // n + rank), bf16),
+            pltpu.VMEM((1, n, width // n), f32),
+            pltpu.VMEM((n * SLOT, HEAD), f32),
+            pltpu.VMEM((n * SLOT, HEAD), f32),
+            pltpu.SemaphoreType.DMA((14,)),
             pltpu.SemaphoreType.DMA((6,)),
             pltpu.SemaphoreType.DMA((6,)),
         ],
         compiler_params=pltpu.CompilerParams(
-            collective_id=0, has_side_effects=True, vmem_limit_bytes=48 * 1024 * 1024
+            collective_id=0, has_side_effects=True, vmem_limit_bytes=60 * 1024 * 1024
         ),
     )(
         lengths,
-        decode_input_rows.astype(f32).reshape(steps, chunks, HEAD),
+        decode_input_rows,
         trig,
         cached_rotated_keys.reshape(length, kv_width),
         cached_value_rows.reshape(length, kv_width),
         base_query_weight,
-        base_key_weight,
-        base_value_weight,
+        base_key_weight.T,
+        base_value_weight.T,
         base_output_weight,
-        query_adapter_down,
-        key_adapter_down,
-        value_adapter_down,
-        query_adapter_up,
+        query_adapter_down.T,
+        key_adapter_down.T,
+        value_adapter_down.T,
+        query_adapter_up.T,
         key_adapter_up,
         value_adapter_up,
-        output_adapter_down,
-        output_adapter_up,
+        output_adapter_down.T,
+        output_adapter_up.T,
     )
     return (
         out.reshape(1, steps, width).astype(bf16),

time: 84.1 us -> 76.1 us (0.905)
  local copies, waits for them, and re-layouts: 10.7 us -> 1.83 us
  other arithmetic: 0.97 us -> 2.98 us
    unnamed x13 -> x0, local copies, waits for them, and re-layouts: 8.92 us -> none
where the time goes in v2:
time: 76.1 us; the launch traced here: 75.7 us
  Pallas kernels  69.6 us (91%)
  other arithmetic  2.98 us (4%)
  local copies, waits for them, and re-layouts  1.83 us (2%)
  between operations  1.3 us (2%)
    pallas_call x1, Pallas kernels, per_device(): pl.pallas_call(functools.partial(decode_kernel, n), out_shape=(jax.ShapeD...  69.6 us

profile of v2, /device:TPU:0, one launch (start us, length us, event | category | flops | bytes accessed | tf_op | source)
XLA Modules:
  0.0 75.7 jit_solution(11065248405396070953)
XLA Ops:
  1.3 0.1 multiply_cosine_fusion
  1.4 0.1 pad_maximum_fusion.1
  1.5 0.6 pad_maximum_fusion.trig_ref
  2.1 69.6 %shard_map.175 = (f32[2,40,128]{2,1,0:T(8,128)}, f32[2,8,128]{2,1,0:T(8,128)}, f32[2,8,128]{2,1,0:T(8,128)}) custom-call(s32[1]{0:T(128)} %copy.20.length_ref, bf16[1,2,5120]{2,1,0:T(2,128)(2,1)} %x_ref.1, f32[2,2,128]{2,1,0:T(2,128)} %pad_maximum_fusion.trig_ref, bf16[2048,1024]{1,0:T(8,128)(2,1)} %bitcast.16, bf16[2048,1024]{1,0:T(8,128)(2,1)} %bitcast.17, ...), custom_call_target="tpu_custom_call" | custom-call | tf_op jit(solution)/shard_map/pallas_call | solution.py:574
  71.7 0.8 %convert_element_type.50 = bf16[2,40,128]{2,1,0:T(8,128)(2,1)S(1)} convert(f32[2,40,128]{2,1,0:T(8,128)} %get-tuple-element.6) | non-fusion elementwise | flops 10240 | bytes 61440 | tf_op jit(solution)/shard_map/convert_element_type | solution.py:635
  72.5 0.6 convert_element_type.51
  73.1 0.7 convert_element_type.52
  73.8 0.6 convert_element_type.53
  74.4 0.7 convert_element_type.54
  75.1 0.6 convert_element_type.55
  (2 shorter events, 0.0 us)

commit v3 on v2

--- a/solution.py
+++ b/solution.py
@@ -214,6 +214,7 @@
     load_sem,
     send_sem,
     recv_sem,
+    cols_sem,
 ):
     me = lax.axis_index("fsdp")
     chunks = x_ref.shape[2] // HEAD
@@ -278,27 +279,14 @@
             in_send[pl.ds(d * SLOT + 3 * t, 3), :] = rows_in[pl.ds(t * chunks + first, 3), :]
     pl.semaphore_wait(barrier, n - 1)
 
-    def exchange(which, source_of, target):
-        def send(i, carry):
-            peer = lax.rem(me + i, n)
-            pltpu.make_async_remote_copy(
-                src_ref=source_of(peer),
-                dst_ref=target.at[me],
-                send_sem=send_sem.at[which],
-                recv_sem=recv_sem.at[which],
-                device_id={"fsdp": peer},
-                device_id_type=pl.DeviceIdType.MESH,
-            ).start()
-            return carry
-
-        lax.fori_loop(1, n, send, 0)
-
     def arrive(which, target):
         whole = target.at[pl.ds(0, n - 1)]
         pltpu.make_async_copy(whole, whole, recv_sem.at[which]).wait()
         pltpu.make_async_copy(whole, whole, send_sem.at[which]).wait()
 
     odd = lax.rem(me, 2)
+    own_pair = me // 2
+    sibling = me + 1 - 2 * odd
     lane = lax.broadcasted_iota(jnp.int32, (KVHEADS, HEAD), 1)
 
     def step_body(step, carry):
@@ -322,8 +310,20 @@
         columns = jnp.concatenate([stream, low[:, : 3 * rank]], axis=1).astype(jnp.bfloat16)
         cols_send[...] = columns
         cols_got[me] = columns
-        exchange(1, lambda peer: cols_send, cols_got)
-        arrive(1, cols_got)
+
+        def send_columns(i, carry):
+            peer = lax.rem(me + i, n)
+            pltpu.make_async_remote_copy(
+                src_ref=cols_send,
+                dst_ref=cols_got.at[me],
+                send_sem=send_sem.at[1],
+                recv_sem=cols_sem.at[me],
+                device_id={"fsdp": peer},
+                device_id_type=pl.DeviceIdType.MESH,
+            ).start()
+            return carry
+
+        lax.fori_loop(1, n, send_columns, 0)
 
         @pl.when(step == 0)
         def _():
@@ -334,11 +334,15 @@
         pair = jnp.zeros((n, HEAD), jnp.float32)
         squares = jnp.zeros((n, 1), jnp.float32)
         for i in range(n // 2):
-            features = pl.ds(i * 2 * share, 2 * share)
+            both = lax.rem(own_pair + i, n // 2)
+            for sender in (sibling,) if i == 0 else (2 * both, 2 * both + 1):
+                landed = cols_got.at[sender]
+                pltpu.make_async_copy(landed, landed, cols_sem.at[sender]).wait()
+            features = pl.ds(pl.multiple_of(both * 2 * share, 2 * share), 2 * share)
             left = jnp.concatenate(
                 [
-                    cols_got[2 * i].astype(jnp.float32)[:, :share],
-                    cols_got[2 * i + 1].astype(jnp.float32)[:, :share],
+                    cols_got[2 * both].astype(jnp.float32)[:, :share],
+                    cols_got[2 * both + 1].astype(jnp.float32)[:, :share],
                 ],
                 axis=1,
             )
@@ -351,6 +355,8 @@
                 (((1,), (1,)), ((), ())),
                 preferred_element_type=jnp.float32,
             )
+        sent = cols_got.at[pl.ds(0, n - 1)]
+        pltpu.make_async_copy(sent, sent, send_sem.at[1]).wait()
         inverse = lax.rsqrt(squares / (chunks * HEAD) + EPSILON)
         low = jnp.sum(cols_got[...].astype(jnp.float32), axis=0)[:, share:].astype(jnp.bfloat16)
 
@@ -455,16 +461,29 @@
         mid = lax.dot_general(
             mixed, down_o[...], (((1,), (1,)), ((), ())), preferred_element_type=jnp.float32
         )
-        for i in range(n // 2):
+        for i in range(1, n // 2 + 1):
+            both = lax.rem(own_pair + i, n // 2)
             piece = jnp.dot(
-                mixed, wo[:, pl.ds(i * 2 * share, 2 * share)], preferred_element_type=jnp.float32
-            )
-            part_send[2 * i] = jnp.concatenate([piece[:, :share], mid], axis=1).astype(jnp.bfloat16)
-            part_send[2 * i + 1] = jnp.concatenate([piece[:, share:], mid], axis=1).astype(
+                mixed,
+                wo[:, pl.ds(pl.multiple_of(both * 2 * share, 2 * share), 2 * share)],
+                preferred_element_type=jnp.float32,
+            )
+            part_send[2 * both] = jnp.concatenate([piece[:, :share], mid], axis=1).astype(
                 jnp.bfloat16
             )
+            part_send[2 * both + 1] = jnp.concatenate([piece[:, share:], mid], axis=1).astype(
+                jnp.bfloat16
+            )
+            for peer in (sibling,) if i == n // 2 else (2 * both, 2 * both + 1):
+                pltpu.make_async_remote_copy(
+                    src_ref=part_send.at[peer],
+                    dst_ref=part_got.at[me],
+                    send_sem=send_sem.at[4],
+                    recv_sem=recv_sem.at[4],
+                    device_id={"fsdp": peer},
+                    device_id_type=pl.DeviceIdType.MESH,
+                ).start()
         part_got[me] = part_send[me]
-        exchange(4, lambda peer: part_send.at[peer], part_got)
         arrive(4, part_got)
         summed = jnp.sum(part_got[...].astype(jnp.float32), axis=0)
         block = rounded(
@@ -608,6 +627,7 @@
             pltpu.SemaphoreType.DMA((14,)),
             pltpu.SemaphoreType.DMA((6,)),
             pltpu.SemaphoreType.DMA((6,)),
+            pltpu.SemaphoreType.DMA((n,)),
         ],
         compiler_params=pltpu.CompilerParams(
             collective_id=0, has_side_effects=True, vmem_limit_bytes=60 * 1024 * 1024

time: 76.1 us -> 75.7 us (level)
  no operation moved by 1% of the time
where the time goes in v3:
time: 75.7 us; the launch traced here: 75.3 us
  Pallas kernels  69.2 us (91%)
  other arithmetic  2.98 us (4%)
  local copies, waits for them, and re-layouts  1.83 us (2%)
  between operations  1.3 us (2%)
    pallas_call x1, Pallas kernels, per_device(): pl.pallas_call(functools.partial(decode_kernel, n), out_shape=(jax.ShapeD...  69.2 us

profile of v3, /device:TPU:0, one launch (start us, length us, event | category | flops | bytes accessed | tf_op | source)
XLA Modules:
  0.0 75.3 jit_solution(2152343872868431930)
XLA Ops:
  1.3 0.1 multiply_cosine_fusion
  1.4 0.1 pad_maximum_fusion.1
  1.5 0.6 pad_maximum_fusion.trig_ref
  2.1 69.2 %shard_map.175 = (f32[2,40,128]{2,1,0:T(8,128)}, f32[2,8,128]{2,1,0:T(8,128)}, f32[2,8,128]{2,1,0:T(8,128)}) custom-call(s32[1]{0:T(128)} %copy.20.length_ref, bf16[1,2,5120]{2,1,0:T(2,128)(2,1)} %x_ref.1, f32[2,2,128]{2,1,0:T(2,128)} %pad_maximum_fusion.trig_ref, bf16[2048,1024]{1,0:T(8,128)(2,1)} %bitcast.16, bf16[2048,1024]{1,0:T(8,128)(2,1)} %bitcast.17, ...), custom_call_target="tpu_custom_call" | custom-call | tf_op jit(solution)/shard_map/pallas_call | solution.py:593
  71.3 0.8 %convert_element_type.50 = bf16[2,40,128]{2,1,0:T(8,128)(2,1)S(1)} convert(f32[2,40,128]{2,1,0:T(8,128)} %get-tuple-element.6) | non-fusion elementwise | flops 10240 | bytes 61440 | tf_op jit(solution)/shard_map/convert_element_type | solution.py:655
  72.1 0.6 convert_element_type.51
  72.7 0.7 convert_element_type.52
  73.4 0.6 convert_element_type.53
  74.0 0.7 convert_element_type.54
  74.7 0.6 convert_element_type.55
  (2 shorter events, 0.0 us)
